TPU v7x, 256 devices: a whole 4x4x8 slice. The times are simulated.
256 devices in a mesh: row: 64 (over y, z, core), col: 4 (over x).
Axes of the slice: x: 4, y: 4, z: 8, core: 2. Of those that a mesh axis runs over, the one named last changes fastest.
Arguments:
- diag_block: float32 [1024, 1024], P('row', 'col'), may hold values from -3 to 3, as said below
- block_rhs: float32 [1024, 512], P('row', 'col'), may hold values from -6 to 6
- panel: float32 [262144, 1024], P('row', 'col'), may hold values from -0.1875 to 0.1875
- trailing_rhs: float32 [262144, 512], P('row', 'col'), may hold values from -6 to 6
Outputs:
- solved: float32 [1024, 512], P('row', 'col')
- trailing: float32 [262144, 512], P('row', 'col')
Inputs may be any that keep to these rules, and one draw needn't show every extreme that they name: diag_block is zero above its diagonal; its diagonal entries lie between 1.5 and 3.
All inputs are finite; a program needn't handle non-finite values.
Results may differ from a plain program's by a relative error of at most 0.000096.
Values sent between devices are 32-bit elements; how exact they have to be, the bound alone decides.
No kernel may reach another device: no remote copies, remote signals or barrier semaphores. Data moves between devices by JAX's collectives and lax.ppermute only.
A program may use at most 128 MiB of HBM per device.

v0:
```python
import jax
import jax.numpy as jnp
from jax import lax
from jax.sharding import PartitionSpec as P


def per_device(diag_block, block_rhs, panel, trailing_rhs):
    row_part = lax.all_gather(diag_block, "col", axis=1, tiled=True)
    factor = lax.all_gather(row_part, "row", axis=0, tiled=True)
    local_rhs = lax.all_gather(block_rhs, "col", axis=1, tiled=True)
    gathered = lax.all_gather(local_rhs, "row", axis=0, tiled=True)
    solved_all = lax.linalg.triangular_solve(factor, gathered, left_side=True, lower=True)
    stripe = block_rhs.shape[0]
    rhs_width = trailing_rhs.shape[1]
    row_start = lax.axis_index("row") * stripe
    col_start = lax.axis_index("col") * rhs_width
    own_solved = lax.dynamic_slice_in_dim(solved_all, col_start, rhs_width, 1)
    solved_out = lax.dynamic_slice_in_dim(own_solved, row_start, stripe, 0)
    panel_width = panel.shape[1]
    block_start = lax.axis_index("col") * panel_width
    needed = lax.dynamic_slice_in_dim(solved_all, block_start, panel_width, 0)
    partial_value = jnp.dot(
        panel, needed, preferred_element_type=jnp.float32, precision=lax.Precision.HIGHEST
    )
    summed = lax.psum_scatter(partial_value, "col", scatter_dimension=1, tiled=True)
    trailing = trailing_rhs - summed
    return (solved_out, trailing)


def solution(mesh):
    in_specs = (P("row", "col"), P("row", "col"), P("row", "col"), P("row", "col"))
    out_specs = (P("row", "col"), P("row", "col"))
    return jax.shard_map(
        per_device, mesh=mesh, in_specs=in_specs, out_specs=out_specs, check_vma=False
    )
```

profile of v0, /device:TPU:6, one launch (start us, length us, event | category | flops | bytes accessed | tf_op | source)
XLA Modules:
  0.0 334.4 jit_solution(12611649565296429637)
XLA Ops:
  7.2 13.1 %all_gather.12 = f32[16,1024]{1,0:T(8,128)} all-gather(f32[16,256]{1,0:T(8,128)} %param.4), channel_id=1, replica_groups=mesh['row'=64,'col'=4] {'col'}, dimensions={1}, use_global_device_ids=true | all-gather | bytes 81920 | tf_op jit(solution)/shard_map/all_gather | solution.py:8
  20.4 12.6 %all_gather.14 = f32[16,512]{1,0:T(8,128)} all-gather(f32[16,128]{1,0:T(8,128)} %param.5), channel_id=1, replica_groups=mesh['row'=64,'col'=4] {'col'}, dimensions={1}, use_global_device_ids=true | all-gather | bytes 40960 | tf_op jit(solution)/shard_map/all_gather | solution.py:10
  33.1 68.8 %all-gather.3.cloned.1.call-done = f32[1024,1024]{1,0:T(8,128)} async-done(((f32[16,1024]{1,0:T(8,128)}), f32[1024,1024]{1,0:T(8,128)}) %all-gather.3.cloned.1.call-update) | async-done | bytes 4194320 | tf_op jit(solution)/shard_map/all_gather | solution.py:9
  101.9 4.7 %fusion = f32[1024,1024]{1,0:T(8,128)} fusion(f32[1024,1024]{1,0:T(8,128)} %all-gather.3.cloned.1.call-done), kind=kLoop, calls=%fused_computation.4 | loop fusion | flops 2097152 | bytes 8388608 | tf_op jit(solution)/shard_map/triangular_solve | solution.py:12
  106.6 23.1 %while.1 = (s32[]{:T(128)}, f32[1024,1024]{1,0:T(8,128)}, s32[8,2]{0,1:T(2,128)S(1)}, f32[8,128,128]{2,1,0:T(8,128)S(1)}, s32[]{:T(128)}) while((s32[]{:T(128)}, f32[1024,1024]{1,0:T(8,128)}, s32[8,2]{0,1:T(2,128)S(1)}, f32[8,128,128]{2,1,0:T(8,128)S(1)}, s32[]{:T(128)}) %tuple.46), condition=%wide.while_cond, body=%wide.while_body.sunk | while | flops 2 | bytes 131181 | solution.py:12
  107.2 2.3 bitcast_dynamic-update-slice_fusion.2
  109.6 0.5 fusion.50
  110.1 2.3 bitcast_dynamic-update-slice_fusion.2
  112.5 0.5 fusion.50
  113.0 2.3 bitcast_dynamic-update-slice_fusion.2
  115.4 0.5 fusion.50
  115.9 2.3 bitcast_dynamic-update-slice_fusion.2
  118.8 2.3 bitcast_dynamic-update-slice_fusion.2
  121.7 2.3 bitcast_dynamic-update-slice_fusion.2
  124.6 2.3 bitcast_dynamic-update-slice_fusion.2
  127.5 2.2 bitcast_dynamic-update-slice_fusion.2
  129.7 78.6 %custom-call.3 = f32[8,128,128]{1,2,0:T(8,128)S(1)} custom-call(f32[8,128,128]{2,1,0:T(8,128)S(1)} %get-tuple-element.9), custom_call_target="InvertDiagBlocksLowerTriangular" | custom-call | tf_op jit(solution)/shard_map/triangular_solve | solution.py:12
  208.3 1.6 constant_dynamic-update-slice_fusion.17
  209.9 1.4 convolution_subtract_fusion.3
  211.8 1.3 convolution_subtract_fusion.2
  213.6 1.6 convolution_subtract_fusion.5
  215.6 1.7 convolution_subtract_fusion.6
  217.8 1.9 convolution_subtract_fusion.1
  220.1 2.0 convolution_subtract_fusion.4
  222.6 2.5 convolution_subtract_fusion
  225.5 1.3 copy-done.2
  226.8 16.4 %convolution_bitcast_fusion = f32[4096,512]{0,1:T(8,128)} fusion(f32[4096,256]{1,0:T(8,128)S(1)} %copy-done, f32[1024,512]{1,0:T(8,128)S(1)} %convolution_dynamic-update-slice_fusion, s32[]{:T(128)S(6)} %select_n.17), kind=kOutput, calls=%fused_computation.2 | convolution fusion | flops 6442450944 | bytes 13107204 | tf_op jit(solution)/shard_map/dot_general | solution.py:22
  243.2 1.9 copy.6
  245.1 1.4 dynamic_slice.7
  246.5 75.3 %reduce-scatter.2.cloned.1.call-done = f32[4096,128]{0,1:T(8,128)} async-done(((f32[4096,512]{0,1:T(8,128)}), f32[4096,128]{0,1:T(8,128)}) %reduce-scatter.2.cloned.1.call-update) | async-done | bytes 2097168 | tf_op jit(solution)/shard_map/reduce_scatter | solution.py:25
  321.8 3.2 sub.3
  325.0 2.9 copy.7
  (35 shorter events, 6.6 us)
Async XLA Ops:
  7.2 94.7 %all-gather.3.cloned.1.call-start = ((), (), s32[]{:S(2)}) async-start(), calls=%async_computation.1 | async-start | bytes 4259840 | tf_op jit(solution)/shard_map/all_gather | solution.py:9
  20.4 188.0 %all-gather.5.cloned.1.call-start = ((), (), s32[]{:S(2)}) async-start(), calls=%async_computation.2 | async-start | bytes 2129920 | tf_op jit(solution)/shard_map/all_gather | solution.py:11
  33.0 288.8 %reduce-scatter.2.cloned.1.call-start = ((), (), s32[]{:S(2)}) async-start(), calls=%async_computation.3 | async-start | bytes 10485760 | tf_op jit(solution)/shard_map/reduce_scatter | solution.py:25
  208.3 3.4 %copy-start.1 = (f32[1024,512]{1,0:T(8,128)S(1)}, f32[1024,512]{1,0:T(8,128)}, u32[]{:S(2)}) copy-start(f32[1024,512]{1,0:T(8,128)} %all-gather.5.cloned.1.call-done) | copy-start | bytes 6291460
  222.1 4.7 %copy-start = (f32[4096,256]{1,0:T(8,128)S(1)}, f32[4096,256]{1,0:T(8,128)}, u32[]{:S(2)}) copy-start(f32[4096,256]{1,0:T(8,128)} %param.6) | copy-start | bytes 12582916
  225.5 1.3 copy-start.2
Sparse Core Ops, SparseCore 0:
  20.5 81.3 all-gather.2
  104.7 74.9 all-gather.4
  243.3 78.4 reduce-scatter.1
where the time goes:
time: 338 us; the launch traced here: 334 us
  waiting for transfers between devices  144 us (43%)
  other arithmetic  86.5 us (26%)
  matrix products  33.4 us (10%)
  local copies, waits for them, and re-layouts  30.5 us (9%)
  blocking collectives  25.7 us (8%)
  between operations  14 us (4%)
    another operation x3, other arithmetic, per_device(): lax.linalg.triangular_solve(factor, gathered, left_side=True, lower=True)  83.3 us
    reduce_scatter x1, waiting for transfers between devices, per_device(): lax.psum_scatter(partial_value, 'col', scatter_dimension=1, tiled=True)  75.3 us
    all_gather x1, waiting for transfers between devices, per_device(): factor = lax.all_gather(row_part, 'row', axis=0, tiled=True)  68.8 us
    another operation x24, local copies, waits for them, and re-layouts  23 us
    another operation x15, matrix products, per_device(): lax.linalg.triangular_solve(factor, gathered, left_side=True, lower=True)  17 us
    dot_general x1, matrix products, per_device(): jnp.dot(panel, needed, preferred_element_type=jnp.float32, precision=lax....  16.4 us
    all_gather x1, blocking collectives, per_device(): row_part = lax.all_gather(diag_block, 'col', axis=1, tiled=True)  13.1 us
    all_gather x1, blocking collectives, per_device(): local_rhs = lax.all_gather(block_rhs, 'col', axis=1, tiled=True)  12.6 us
  transfers between devices with their start and end apart: 3, of which 2 were waited for; matrix products, arithmetic and copies ran while one was open for 33% of the time, Pallas kernels for 0%

commit v1 on v0

v1 whole, which is shorter than its diff:
```python
import jax
import jax.numpy as jnp
from jax import lax
from jax.experimental import pallas as pl
from jax.experimental.pallas import tpu as pltpu
from jax.sharding import PartitionSpec as P

NY, NZ, NC = 4, 8, 2
HALVES = 2
MIB = 1024 * 1024


def mm(a, b):
    return jnp.dot(a, b, preferred_element_type=jnp.float32, precision=lax.Precision.HIGHEST)


def tiny_inverses(blocks):
    n = len(blocks)
    lane = lax.broadcasted_iota(jnp.int32, (16, 128), 1)
    row = lax.broadcasted_iota(jnp.int32, (16, 128), 0)
    seg = lane // 16
    packed = []
    for a in blocks:
        p = jnp.zeros((16, 128), jnp.float32)
        for s in range(8):
            p = jnp.where(seg == s, a[16 * s : 16 * s + 16, :], p)
        packed.append(p)
    p = jnp.concatenate(packed, axis=0)
    lane_n = lax.broadcasted_iota(jnp.int32, (16 * n, 128), 1)
    r = jnp.where(lane == seg * 16 + row, 1.0, 0.0).astype(jnp.float32)
    r = jnp.broadcast_to(r[None], (n, 16, 128))
    row3 = lax.broadcasted_iota(jnp.int32, (n, 16, 128), 1)
    for j in range(16):
        idx = (lane_n // 16) * 16 + j
        column = jnp.take_along_axis(p, idx, axis=1).reshape(n, 16, 128)
        w = r[:, j : j + 1, :] / column[:, j : j + 1, :]
        r = jnp.where(row3 > j, r - column * w, jnp.where(row3 == j, w, r))
    return [
        jnp.concatenate([jnp.where(seg == s, r[b], 0.0) for s in range(8)], axis=0) for b in range(n)
    ]


def grow(a, d, s):
    i = lax.broadcasted_iota(jnp.int32, a.shape, 0)
    k = lax.broadcasted_iota(jnp.int32, a.shape, 1)
    off = (i // (2 * s) == k // (2 * s)) & ((i // s) % 2 == 1) & ((k // s) % 2 == 0)
    return d - mm(d, mm(jnp.where(off, a, 0.0), d))


BELOW = ((1, 0), (2, 0), (2, 1), (3, 0), (3, 1), (3, 2))


def split(a):
    high = a.astype(jnp.bfloat16)
    return high, (a - high.astype(jnp.float32)).astype(jnp.bfloat16)


def solve_kernel(where, low_own, low_other, *refs):
    own4, other4, (x_ref, xh, xl, dinv, rest) = refs[:4], refs[4:8], refs[8:]
    first = where[0] == 0

    def rows(own, other):
        a = jnp.where(first, own, other)
        b = jnp.where(first, other, own)
        return jnp.stack([a, b], axis=1).reshape(256, own.shape[-1])

    def lower(k, j):
        n = BELOW.index((k, j))
        return rows(low_own[:, n], low_other[:, n])

    for n in range(NY):
        rest[(where[1] + n) % NY] = rows(own4[n][...], other4[n][...])

    def diagonal(k):
        return rest[k, :, :256]

    blocks = []
    for k in range(NY):
        t = diagonal(k)
        blocks += [t[:128, :128], t[128:, 128:]]
    ds = tiny_inverses(blocks)
    for s in (16, 32, 64):
        ds = [grow(a, d, s) for a, d in zip(blocks, ds)]
    for k in range(NY):
        da, db = ds[2 * k], ds[2 * k + 1]
        dinv[k, :128, :128] = da
        dinv[k, :128, 128:] = jnp.zeros((128, 128), jnp.float32)
        dinv[k, 128:, :128] = -mm(db, mm(diagonal(k)[128:, :128], da))
        dinv[k, 128:, 128:] = db
    for k in range(NY):
        r = rest[k, :, 256:]
        for j in range(k):
            r = r - mm(lower(k, j), x_ref[256 * j : 256 * j + 256, :])
        x = mm(dinv[k], r)
        x_ref[256 * k : 256 * k + 256, :] = x
        xh[k], xl[k] = split(x)


def solve(where, low_own, low_other, rests, rests_other):
    vmem = pl.BlockSpec(memory_space=pltpu.VMEM)
    return pl.pallas_call(
        solve_kernel,
        out_shape=[jax.ShapeDtypeStruct((1024, 512), jnp.float32)]
        + [jax.ShapeDtypeStruct((NY, 256, 512), jnp.bfloat16)] * 2,
        in_specs=[pl.BlockSpec(memory_space=pltpu.SMEM)] + [vmem] * 10,
        out_specs=[vmem] * 3,
        scratch_shapes=[pltpu.VMEM((NY, 256, 256), jnp.float32), pltpu.VMEM((NY, 256, 768), jnp.float32)],
        compiler_params=pltpu.CompilerParams(vmem_limit_bytes=12 * MIB),
        cost_estimate=pl.CostEstimate(flops=4 * 10**9, bytes_accessed=8 * MIB, transcendentals=0),
    )(where, low_own, low_other, *rests, *rests_other)


def product_kernel(col_ref, own, left, right, far, xh, xl, *refs):
    outs, parts = refs[:4], refs[4]
    acc = jnp.zeros((own.shape[0], 512), jnp.float32)
    for piece, shift in ((own, 0), (left, 3), (right, 1), (far, 2)):
        k = (col_ref[0] + shift) % 4
        ah, al = split(piece[...])
        bh, bl = xh[k], xl[k]
        for a, b in ((ah, bh), (ah, bl), (al, bh)):
            acc += jnp.dot(a, b, preferred_element_type=jnp.float32)
    for j in range(4):
        parts[j] = acc[:, 128 * j : 128 * j + 128]
    for k in range(4):
        outs[k][...] = parts[(col_ref[0] + k) % 4]


def product(col, panel, half, pieces, xh, xl):
    n, tile = pieces[0].shape[0], 256
    steps = n // tile
    piece = pl.BlockSpec((tile, 256), lambda i, c: (i, 0))
    full = pl.BlockSpec((4, 256, 512), lambda i, c: (0, 0, 0))
    out = pl.BlockSpec((tile, 128), lambda i, c: (i, 0))
    return pl.pallas_call(
        product_kernel,
        out_shape=[jax.ShapeDtypeStruct((n, 128), jnp.float32)] * 4,
        grid_spec=pltpu.PrefetchScalarGridSpec(
            num_scalar_prefetch=1,
            grid=(steps,),
            in_specs=[pl.BlockSpec((tile, 256), lambda i, c: ((c[0] * HALVES + half) * steps + i, 0))]
            + [piece] * 3
            + [full] * 2,
            out_specs=[out] * 4,
            scratch_shapes=[pltpu.VMEM((4, tile, 128), jnp.float32)],
        ),
        compiler_params=pltpu.CompilerParams(vmem_limit_bytes=16 * MIB),
        cost_estimate=pl.CostEstimate(flops=6 * n * 1024 * 512, bytes_accessed=6 * MIB, transcendentals=0),
    )(col, panel, *pieces, xh, xl)


def finish_kernel(col_ref, rhs, own, left, right, far, *refs):
    out = refs[-1]
    for n, piece in enumerate((own, left, right, far)):

        @pl.when(pl.program_id(0) == n)
        def _():
            out[...] = rhs[...] - piece[...]


def finish(col, rhs, half, pieces, before):
    n = pieces[0].shape[0]

    def block(i, c):
        source = (c[0] + jnp.where(i == 0, 0, jnp.where(i == 1, 3, i - 1))) % 4
        return (source * HALVES + half, 0)

    piece = pl.BlockSpec((n, 128), lambda i, c: (0, 0))
    prior = [] if before is None else [before]
    return pl.pallas_call(
        finish_kernel,
        out_shape=jax.ShapeDtypeStruct(rhs.shape, jnp.float32),
        grid_spec=pltpu.PrefetchScalarGridSpec(
            num_scalar_prefetch=1,
            grid=(4,),
            in_specs=[pl.BlockSpec((n, 128), block)] + [piece] * 4 + [pl.BlockSpec(memory_space=pl.ANY)] * len(prior),
            out_specs=pl.BlockSpec((n, 128), block),
        ),
        input_output_aliases={6: 0} if prior else {},
        compiler_params=pltpu.CompilerParams(vmem_limit_bytes=16 * MIB),
        cost_estimate=pl.CostEstimate(flops=4 * n * 128, bytes_accessed=12 * n * 512, transcendentals=0),
    )(col, rhs, *pieces, *prior)


def z_groups():
    return [[(y * NZ + z) * NC + c for z in range(NZ)] for y in range(NY) for c in range(NC)]


def y_groups():
    return [[(y * NZ + z) * NC + c for y in range(NY)] for z in range(NZ) for c in range(NC)]


def spread(a, axis, n, groups=None):
    return lax.all_to_all(
        jnp.broadcast_to(a[None], (n,) + a.shape), axis, 0, 0, tiled=True, axis_index_groups=groups
    )


def swap_cores(a):
    return lax.ppermute(a, "row", [(i, i ^ 1) for i in range(NY * NZ * NC)])


def shift_y(a, k):
    step = k * NZ * NC
    n = NY * NZ * NC
    return lax.ppermute(a, "row", [(i, (i + step) % n) for i in range(n)])


def send_x(a, k):
    return lax.ppermute(a, "col", [(i, (i + k) % 4) for i in range(4)])


def from_planes(a, y):
    parts = jnp.stack([a, shift_y(a, 3), shift_y(a, 2), shift_y(a, 1)])
    return [lax.dynamic_index_in_dim(parts, (k - y) % NY, 0, keepdims=False) for k in range(NY)]


def per_device(diag_block, block_rhs, panel, trailing_rhs):
    row, col = lax.axis_index("row"), lax.axis_index("col")
    y = row // (NZ * NC)
    quarter = panel.shape[0] // 4

    mine = spread(jnp.concatenate([diag_block, block_rhs], axis=1), "col", 4)
    chunk = panel.shape[0] // (4 * HALVES)
    chunks = [
        [lax.dynamic_slice_in_dim(panel, ((col + k) % 4 * HALVES + h) * chunk, chunk, 0) for k in (1, 3, 2)]
        for h in range(HALVES)
    ]
    mine, chunks = lax.optimization_barrier((mine, chunks))
    moved = [[send_x(p, k) for p, k in zip(c, (1, 3, 2))] for c in chunks]

    diagonal = lax.dynamic_index_in_dim(mine, y, 0, keepdims=False)[:, :256]
    rest = jnp.concatenate([diagonal] + [mine[c, :, 256:] for c in range(4)], axis=1)
    rest = spread(rest, "row", NZ, z_groups())
    low = from_planes(mine[:3, :, :256], y)
    low = jnp.stack([low[k][j] for k, j in BELOW])
    moved[0], rest, low = lax.optimization_barrier((moved[0], rest, low))
    low = spread(low, "row", NZ, z_groups())
    others = [shift_y(rest, k) for k in (3, 2, 1)]
    moved[1], low, others = lax.optimization_barrier((moved[1], low, others))
    rests = [rest] + others
    low_other, rests_other = swap_cores(low), [swap_cores(r) for r in rests]
    where = jnp.stack([row % NC, y]).astype(jnp.int32)
    x, xh, xl = solve(where, low, low_other, rests, rests_other)

    me = jnp.reshape(col, (1,)).astype(jnp.int32)
    parts = [product(me, panel, h, moved[h], xh, xl) for h in range(HALVES)]
    trailing = None
    for h in range(HALVES):
        own, *sent = parts[h]
        far = send_x(sent[1], 2)
        pieces = [own, send_x(sent[0], 1), send_x(sent[2], 3), far]
        trailing = finish(me, trailing_rhs, h, pieces, trailing)
    stripe = lax.dynamic_slice(x, (row * block_rhs.shape[0], col * 128), block_rhs.shape)
    return (stripe, trailing)


def solution(mesh):
    specs = (P("row", "col"),) * 4
    return jax.shard_map(per_device, mesh=mesh, in_specs=specs, out_specs=(P("row", "col"),) * 2, check_vma=False)
```

time: 338 us -> 138 us (0.41)
  other arithmetic: 86.5 us -> 0.83 us
  waiting for transfers between devices: 144 us -> 59.4 us
  starting transfers between devices: 0.12 us -> 43.9 us
  matrix products: 33.4 us -> 0 us
  blocking collectives: 25.7 us -> 0 us
  Pallas kernels: 0 us -> 20.5 us
  local copies, waits for them, and re-layouts: 30.5 us -> 12.3 us
  between operations: 14 us -> 0.79 us
    another operation x3 -> x2, other arithmetic: 83.3 us -> 0.09 us  [the longest x1 0.07 us: per_device(): where = jnp.stack([row % NC, y]).astype(jnp.int32)]
    reduce_scatter x1 -> x0, waiting for transfers between devices: 75.3 us -> none  [per_device(): lax.psum_scatter(partial_value, 'col', scatter_dimension=1, tiled=True)]
    all_gather x2 -> x0, waiting for transfers between devices: 68.8 us -> none  [the longest x1 68.8 us: per_device(): factor = lax.all_gather(row_part, 'row', axis=0, tiled=True)]
    ppermute x0 -> x23, waiting for transfers between devices: none -> 58.9 us  [the longest x12 51.9 us: send_x(): return lax.ppermute(a, 'col', [(i, (i + k) % 4) for i in range(4)])]
    all_gather x2 -> x0, blocking collectives: 25.7 us -> none  [the longest x1 13.1 us: per_device(): row_part = lax.all_gather(diag_block, 'col', axis=1, tiled=True)]
    ppermute x0 -> x23, starting transfers between devices: none -> 23 us  [the longest x12 14.4 us: send_x(): return lax.ppermute(a, 'col', [(i, (i + k) % 4) for i in range(4)])]
    another operation x25 -> x2, local copies, waits for them, and re-layouts: 23 us -> 0.02 us  [the longest x1 0.01 us: per_device(): low = jnp.stack([low[k][j] for k, j in BELOW])]
    all_to_all x0 -> x3, starting transfers between devices: none -> 20.9 us  [spread(): lax.all_to_all(jnp.broadcast_to(a[None], (n,) + a.shape), axis, 0, 0, til...]
  transfers between devices with their start and end apart: 3 -> 26, of which waited for: 2 -> 14; matrix products, arithmetic and copies ran while one was open for 33% -> 4% of each run, Pallas kernels for 0% -> 4%
where the time goes in v1:
time: 138 us
  waiting for transfers between devices  59.4 us (43%)
  starting transfers between devices  43.9 us (32%)
  Pallas kernels  20.5 us (15%)
  local copies, waits for them, and re-layouts  12.3 us (9%)
    ppermute x12, waiting for transfers between devices, send_x(): return lax.ppermute(a, 'col', [(i, (i + k) % 4) for i in range(4)])  51.9 us
    all_to_all x3, starting transfers between devices, spread(): lax.all_to_all(jnp.broadcast_to(a[None], (n,) + a.shape), axis, 0, 0, til...  20.9 us
    ppermute x12, starting transfers between devices, send_x(): return lax.ppermute(a, 'col', [(i, (i + k) % 4) for i in range(4)])  14.4 us
    pallas_call x1, Pallas kernels, solve(): pl.pallas_call(solve_kernel, out_shape=[jax.ShapeDtypeStruct((1024, 512),...  10.6 us
    ppermute x6, starting transfers between devices, shift_y(): return lax.ppermute(a, 'row', [(i, (i + step) % n) for i in range(n)])  7.55 us
    pallas_call x2, Pallas kernels, product(): pl.pallas_call(product_kernel, out_shape=[jax.ShapeDtypeStruct((n, 128),...  5.73 us
    unnamed x35, local copies, waits for them, and re-layouts  5.33 us
    pallas_call x2, Pallas kernels, finish(): pl.pallas_call(finish_kernel, out_shape=jax.ShapeDtypeStruct(rhs.shape, j...  4.23 us
  transfers between devices with their start and end apart: 26, of which 14 were waited for; matrix products, arithmetic and copies ran while one was open for 4% of the time, Pallas kernels for 4%

profile of v1, /device:TPU:6, one launch (start us, length us, event | category | flops | bytes accessed | tf_op | source)
XLA Modules:
  0.0 137.8 jit_solution(14062457191819679420)
XLA Ops:
  2.0 5.5 %all-to-all-start = ((f32[4,16,384]{2,1,0:T(8,128)}), f32[4,16,384]{2,1,0:T(8,128)S(1)}, u32[]{:S(2)}, u32[]{:S(2)}) async-start(f32[4,16,384]{2,1,0:T(8,128)} %broadcast_in_dim.6), calls=%async_computation | async-start | bytes 196608 | tf_op jit(solution)/shard_map/all_to_all | solution.py:193
  7.5 3.2 %constant_dynamic-slice_fusion = (f32[512,256]{1,0:T(8,128)}, f32[512,256]{1,0:T(8,128)}, f32[512,256]{1,0:T(8,128)}, f32[512,256]{1,0:T(8,128)S(1)}, f32[512,256]{1,0:T(8,128)S(1)}, /*index=5*/f32[512,256]{1,0:T(8,128)}) fusion(f32[4096,256]{1,0:T(8,128)} %own.3, s32[]{:T(128)S(6)} %select_n.89, s32[]{:T(128)S(6)} %select_n.88, s32[]{:T(128)S(6)} %select_n.87, ...), kind=kLoop, calls=%fused_computation.20 | loop fusion | bytes 6291480 | tf_op jit(solution)/shard_map/dynamic_slice | solution.py:225
  12.2 2.4 %collective-permute-start.6 = (f32[3,16,256]{2,1,0:T(8,128)S(1)}, f32[3,16,256]{2,1,0:T(8,128)S(1)}, u32[]{:S(2)}, u32[]{:S(2)}) collective-permute-start(f32[3,16,256]{2,1,0:T(8,128)S(1)} %get-tuple-element.69), channel_id=1, source_target_pairs={{0,192},{4,196},{8,200},{12,204},{16,208},{20,212},{24,216},{28,22... | collective-permute-start | bytes 147464 | tf_op jit(solution)/shard_map/ppermute | solution.py:205
  14.5 1.3 collective-permute-start.7
  16.6 8.5 %all-to-all-start.1 = ((f32[8,16,768]{2,1,0:T(8,128)}), f32[8,16,768]{2,1,0:T(8,128)S(1)}, u32[]{:S(2)}, u32[]{:S(2)}) async-start(f32[8,16,768]{2,1,0:T(8,128)} %broadcast_in_dim.7), calls=%async_computation.1 | async-start | bytes 786432 | tf_op jit(solution)/shard_map/all_to_all | solution.py:193
  25.1 2.1 %collective-permute-start.3 = (f32[512,256]{1,0:T(8,128)}, f32[512,256]{1,0:T(8,128)S(1)}, u32[]{:S(2)}, u32[]{:S(2)}) collective-permute-start(f32[512,256]{1,0:T(8,128)} %get-tuple-element.35), channel_id=1, source_target_pairs={{0,1},{1,2},{2,3},{3,0},{4,5},{5,6},{6,7},{7,4},{8,9},{9,10},{10,1... | collective-permute-start | bytes 1572872 | tf_op jit(solution)/shard_map/ppermute | solution.py:209
  27.2 2.0 %collective-permute-start.5 = (f32[512,256]{1,0:T(8,128)S(1)}, f32[512,256]{1,0:T(8,128)S(1)}, u32[]{:S(2)}, u32[]{:S(2)}) collective-permute-start(f32[512,256]{1,0:T(8,128)S(1)} %get-tuple-element.37), channel_id=1, source_target_pairs={{0,2},{1,3},{2,0},{3,1},{4,6},{5,7},{6,4},{7,5},{8,10},{9,11},{10,... | collective-permute-start | bytes 1572872 | tf_op jit(solution)/shard_map/ppermute | solution.py:209
  29.3 10.8 %collective-permute-done.3.left = f32[512,256]{1,0:T(8,128)S(1)} collective-permute-done((f32[512,256]{1,0:T(8,128)}, f32[512,256]{1,0:T(8,128)S(1)}, u32[]{:S(2)}, u32[]{:S(2)}) %collective-permute-start.3) | collective-permute-done | bytes 524320 | tf_op jit(solution)/shard_map/ppermute | solution.py:209
  40.2 10.3 %collective-permute-done.4.right = f32[512,256]{1,0:T(8,128)S(1)} collective-permute-done((f32[512,256]{1,0:T(8,128)S(1)}, f32[512,256]{1,0:T(8,128)S(1)}, u32[]{:S(2)}, u32[]{:S(2)}) %collective-permute-start.4) | collective-permute-done | bytes 524320 | tf_op jit(solution)/shard_map/ppermute | solution.py:209
  50.5 1.0 broadcast_in_dim.8
  51.5 6.9 %all-to-all-start.2 = ((f32[8,6,16,256]{3,2,1,0:T(8,128)}), f32[8,6,16,256]{3,2,1,0:T(8,128)S(1)}, u32[]{:S(2)}, u32[]{:S(2)}) async-start(f32[8,6,16,256]{3,2,1,0:T(8,128)} %broadcast_in_dim.8), calls=%async_computation.2 | async-start | bytes 1572864 | tf_op jit(solution)/shard_map/all_to_all | solution.py:193
  58.9 1.5 %collective-permute-start.1 = (f32[512,256]{1,0:T(8,128)}, f32[512,256]{1,0:T(8,128)S(1)}, u32[]{:S(2)}, u32[]{:S(2)}) collective-permute-start(f32[512,256]{1,0:T(8,128)} %get-tuple-element.33), channel_id=1, source_target_pairs={{0,3},{1,0},{2,1},{3,2},{4,7},{5,4},{6,5},{7,6},{8,11},{9,8},{10,9... | collective-permute-start | bytes 1572872 | tf_op jit(solution)/shard_map/ppermute | solution.py:209
  61.1 1.7 %collective-permute-start.10 = (f32[8,16,768]{2,1,0:T(8,128)}, f32[8,16,768]{2,1,0:T(8,128)}, u32[]{:S(2)}, u32[]{:S(2)}) collective-permute-start(f32[8,16,768]{2,1,0:T(8,128)} %copy-done.4), channel_id=1, source_target_pairs={{0,128},{4,132},{8,136},{12,140},{16,144},{20,148},{24,152},{28,15... | collective-permute-start | bytes 1179656 | tf_op jit(solution)/shard_map/ppermute | solution.py:205
  63.0 14.9 %collective-permute-done.left = f32[512,256]{1,0:T(8,128)S(1)} collective-permute-done((f32[512,256]{1,0:T(8,128)}, f32[512,256]{1,0:T(8,128)S(1)}, u32[]{:S(2)}, u32[]{:S(2)}) %collective-permute-start) | collective-permute-done | bytes 524320 | tf_op jit(solution)/shard_map/ppermute | solution.py:209
  77.8 1.1 collective-permute-start.9
  78.9 2.2 %collective-permute-done.1.right = f32[512,256]{1,0:T(8,128)S(1)} collective-permute-done((f32[512,256]{1,0:T(8,128)}, f32[512,256]{1,0:T(8,128)S(1)}, u32[]{:S(2)}, u32[]{:S(2)}) %collective-permute-start.1) | collective-permute-done | bytes 524320 | tf_op jit(solution)/shard_map/ppermute | solution.py:209
  82.7 3.2 %collective-permute-done.9.refs_1_ = f32[8,16,768]{2,1,0:T(8,128)} collective-permute-done((f32[8,16,768]{2,1,0:T(8,128)}, f32[8,16,768]{2,1,0:T(8,128)}, u32[]{:S(2)}, u32[]{:S(2)}) %collective-permute-start.9) | collective-permute-done | bytes 393248 | tf_op jit(solution)/shard_map/ppermute | solution.py:205
  87.0 1.7 %collective-permute-done.13.refs_4_ = f32[8,16,768]{2,1,0:T(8,128)} collective-permute-done((f32[8,16,768]{2,1,0:T(8,128)}, f32[8,16,768]{2,1,0:T(8,128)}, u32[]{:S(2)}, u32[]{:S(2)}) %collective-permute-start.13) | collective-permute-done | bytes 393248 | tf_op jit(solution)/shard_map/ppermute | solution.py:199
  90.8 1.0 copy-done.5
  92.8 10.6 %shard_map.59 = (f32[1024,512]{1,0:T(8,128)S(1)}, bf16[4,256,512]{2,1,0:T(8,128)(2,1)S(1)}, bf16[4,256,512]{2,1,0:T(8,128)(2,1)S(1)}) custom-call(s32[2]{0:T(128)S(1)} %pad_add_fusion.where, f32[8,6,16,256]{3,2,1,0:T(8,128)S(1)} %all-to-all-done.2.low_own, f32[8,6,16,256]{3,2,1,0:T(8,128)} %collective-permute-done.12.low_other, f32[8,16,768]{2,1,0:T(8,128)S(1)} %copy-done.5, ...), custom_call_target="tpu_custom_call" | custom-call | flops 4000000000 | bytes 8388608 | tf_op jit(solution)/shard_map/pallas_call | solution.py:101
  103.4 2.8 %shard_map.61 = (f32[512,128]{1,0:T(8,128)S(1)}, f32[512,128]{1,0:T(8,128)S(1)}, f32[512,128]{1,0:T(8,128)}, f32[512,128]{1,0:T(8,128)}) custom-call(s32[1]{0:T(128)} %bitcast.17.col_ref, f32[4096,256]{1,0:T(8,128)S(1)} %copy-done, f32[512,256]{1,0:T(8,128)S(1)} %collective-permute-done.3.left, f32[512,256]{1,0:T(8,128)S(1)} %collective-permute-done.4.right, ...), custom_call_target="tpu_custom_call" | custom-call | flops 1610612736 | bytes 6291456 | tf_op jit(solution)/shard_map/pallas_call | solution.py:134
  106.3 3.6 %collective-permute-start.20 = (f32[512,128]{1,0:T(8,128)S(1)}, f32[512,128]{1,0:T(8,128)S(1)}, u32[]{:S(2)}, u32[]{:S(2)}) collective-permute-start(f32[512,128]{1,0:T(8,128)S(1)} %get-tuple-element.59), channel_id=1, source_target_pairs={{0,1},{1,2},{2,3},{3,0},{4,5},{5,6},{6,7},{7,4},{8,9},{9,10},{10,1... | collective-permute-start | bytes 786440 | tf_op jit(solution)/shard_map/ppermute | solution.py:209
  109.8 1.5 %collective-permute-start.22 = (f32[512,128]{1,0:T(8,128)}, f32[512,128]{1,0:T(8,128)}, u32[]{:S(2)}, u32[]{:S(2)}) collective-permute-start(f32[512,128]{1,0:T(8,128)} %get-tuple-element.61), channel_id=1, source_target_pairs={{0,2},{1,3},{2,0},{3,1},{4,6},{5,7},{6,4},{7,5},{8,10},{9,11},{10,... | collective-permute-start | bytes 786440 | tf_op jit(solution)/shard_map/ppermute | solution.py:209
  111.3 2.9 %shard_map.60 = (f32[512,128]{1,0:T(8,128)S(1)}, f32[512,128]{1,0:T(8,128)}, f32[512,128]{1,0:T(8,128)}, f32[512,128]{1,0:T(8,128)}) custom-call(s32[1]{0:T(128)} %bitcast.17.col_ref, f32[4096,256]{1,0:T(8,128)S(1)} %copy-done, f32[512,256]{1,0:T(8,128)S(1)} %collective-permute-done.left, f32[512,256]{1,0:T(8,128)S(1)} %collective-permute-done.1.right, ...), custom_call_target="tpu_custom_call" | custom-call | flops 1610612736 | bytes 6291456 | tf_op jit(solution)/shard_map/pallas_call | solution.py:134
  115.0 1.8 %collective-permute-start.17 = (f32[512,128]{1,0:T(8,128)}, f32[512,128]{1,0:T(8,128)S(1)}, u32[]{:S(2)}, u32[]{:S(2)}) collective-permute-start(f32[512,128]{1,0:T(8,128)} %get-tuple-element.52), channel_id=1, source_target_pairs={{0,1},{1,2},{2,3},{3,0},{4,5},{5,6},{6,7},{7,4},{8,9},{9,10},{10,1... | collective-permute-start | bytes 786440 | tf_op jit(solution)/shard_map/ppermute | solution.py:209
  117.5 4.6 %collective-permute-done.20.left = f32[512,128]{1,0:T(8,128)S(1)} collective-permute-done((f32[512,128]{1,0:T(8,128)S(1)}, f32[512,128]{1,0:T(8,128)S(1)}, u32[]{:S(2)}, u32[]{:S(2)}) %collective-permute-start.20) | collective-permute-done | bytes 262176 | tf_op jit(solution)/shard_map/ppermute | solution.py:209
  122.1 1.3 dynamic_slice.45
  123.4 2.8 %collective-permute-done.21.right = f32[512,128]{1,0:T(8,128)} collective-permute-done((f32[512,128]{1,0:T(8,128)}, f32[512,128]{1,0:T(8,128)}, u32[]{:S(2)}, u32[]{:S(2)}) %collective-permute-start.21) | collective-permute-done | bytes 262176 | tf_op jit(solution)/shard_map/ppermute | solution.py:209
  127.1 2.6 %shard_map.62.refs_0_ = f32[4096,128]{1,0:T(8,128)} custom-call(s32[1]{0:T(128)} %bitcast.17.col_ref, f32[4096,128]{1,0:T(8,128)S(1)} %copy-done.1, f32[512,128]{1,0:T(8,128)S(1)} %copy-done.7, f32[512,128]{1,0:T(8,128)S(1)} %collective-permute-done.20.left, f32[512,128]{1,0:T(8,128)} %collective-permute-done.21.right, f32[512,128]{1,0:T(8,128)} %collective-permute-done.22.far), custom_call_target="tpu_custom_call" | custom-call | flops 262144 | bytes 3145728 | tf_op jit(solution)/shard_map/pallas_call | solution.py:169
  129.8 2.9 %collective-permute-done.17.left = f32[512,128]{1,0:T(8,128)S(1)} collective-permute-done((f32[512,128]{1,0:T(8,128)}, f32[512,128]{1,0:T(8,128)S(1)}, u32[]{:S(2)}, u32[]{:S(2)}) %collective-permute-start.17) | collective-permute-done | bytes 262176 | tf_op jit(solution)/shard_map/ppermute | solution.py:209
  132.7 3.5 %collective-permute-done.18.right = f32[512,128]{1,0:T(8,128)S(1)} collective-permute-done((f32[512,128]{1,0:T(8,128)}, f32[512,128]{1,0:T(8,128)S(1)}, u32[]{:S(2)}, u32[]{:S(2)}) %collective-permute-start.18) | collective-permute-done | bytes 262176 | tf_op jit(solution)/shard_map/ppermute | solution.py:209
  136.2 1.6 %shard_map.63 = f32[4096,128]{1,0:T(8,128)} custom-call(s32[1]{0:T(128)} %bitcast.17.col_ref, f32[4096,128]{1,0:T(8,128)S(1)} %copy-done.1, f32[512,128]{1,0:T(8,128)S(1)} %copy-done.9, f32[512,128]{1,0:T(8,128)S(1)} %collective-permute-done.17.left, f32[512,128]{1,0:T(8,128)S(1)} %collective-permute-done.18.right, ...), custom_call_target="tpu_custom_call", output_to_operand_aliasing={{}: (6, {})} | custom-call | flops 262144 | bytes 3145728 | tf_op jit(solution)/shard_map/pallas_call | solution.py:169
  (72 shorter events, 13.3 us)
Async XLA Ops:
  2.0 9.2 %all-to-all-start = ((f32[4,16,384]{2,1,0:T(8,128)}), f32[4,16,384]{2,1,0:T(8,128)S(1)}, u32[]{:S(2)}, u32[]{:S(2)}) async-start(f32[4,16,384]{2,1,0:T(8,128)} %broadcast_in_dim.6), calls=%async_computation | async-start | bytes 196608 | tf_op jit(solution)/shard_map/all_to_all | solution.py:193
  11.2 15.9 %collective-permute-start.8 = (f32[3,16,256]{2,1,0:T(8,128)S(1)}, f32[3,16,256]{2,1,0:T(8,128)S(1)}, u32[]{:S(2)}, u32[]{:S(2)}) collective-permute-start(f32[3,16,256]{2,1,0:T(8,128)S(1)} %get-tuple-element.69), channel_id=1, source_target_pairs={{0,64},{4,68},{8,72},{12,76},{16,80},{20,84},{24,88},{28,92},{32,9... | collective-permute-start | bytes 147464 | tf_op jit(solution)/shard_map/ppermute | solution.py:205
  12.2 17.0 %collective-permute-start.6 = (f32[3,16,256]{2,1,0:T(8,128)S(1)}, f32[3,16,256]{2,1,0:T(8,128)S(1)}, u32[]{:S(2)}, u32[]{:S(2)}) collective-permute-start(f32[3,16,256]{2,1,0:T(8,128)S(1)} %get-tuple-element.69), channel_id=1, source_target_pairs={{0,192},{4,196},{8,200},{12,204},{16,208},{20,212},{24,216},{28,22... | collective-permute-start | bytes 147464 | tf_op jit(solution)/shard_map/ppermute | solution.py:205
  14.5 14.7 %collective-permute-start.7 = (f32[3,16,256]{2,1,0:T(8,128)S(1)}, f32[3,16,256]{2,1,0:T(8,128)S(1)}, u32[]{:S(2)}, u32[]{:S(2)}) collective-permute-start(f32[3,16,256]{2,1,0:T(8,128)S(1)} %get-tuple-element.69), channel_id=1, source_target_pairs={{0,128},{4,132},{8,136},{12,140},{16,144},{20,148},{24,152},{28,15... | collective-permute-start | bytes 147464 | tf_op jit(solution)/shard_map/ppermute | solution.py:205
  16.6 33.8 %all-to-all-start.1 = ((f32[8,16,768]{2,1,0:T(8,128)}), f32[8,16,768]{2,1,0:T(8,128)S(1)}, u32[]{:S(2)}, u32[]{:S(2)}) async-start(f32[8,16,768]{2,1,0:T(8,128)} %broadcast_in_dim.7), calls=%async_computation.1 | async-start | bytes 786432 | tf_op jit(solution)/shard_map/all_to_all | solution.py:193
  25.1 15.1 %collective-permute-start.3 = (f32[512,256]{1,0:T(8,128)}, f32[512,256]{1,0:T(8,128)S(1)}, u32[]{:S(2)}, u32[]{:S(2)}) collective-permute-start(f32[512,256]{1,0:T(8,128)} %get-tuple-element.35), channel_id=1, source_target_pairs={{0,1},{1,2},{2,3},{3,0},{4,5},{5,6},{6,7},{7,4},{8,9},{9,10},{10,1... | collective-permute-start | bytes 1572872 | tf_op jit(solution)/shard_map/ppermute | solution.py:209
  27.2 23.3 %collective-permute-start.4 = (f32[512,256]{1,0:T(8,128)S(1)}, f32[512,256]{1,0:T(8,128)S(1)}, u32[]{:S(2)}, u32[]{:S(2)}) collective-permute-start(f32[512,256]{1,0:T(8,128)S(1)} %get-tuple-element.36), channel_id=1, source_target_pairs={{0,3},{1,0},{2,1},{3,2},{4,7},{5,4},{6,5},{7,6},{8,11},{9,8},{10,9... | collective-permute-start | bytes 1572872 | tf_op jit(solution)/shard_map/ppermute | solution.py:209
  27.2 23.3 %collective-permute-start.5 = (f32[512,256]{1,0:T(8,128)S(1)}, f32[512,256]{1,0:T(8,128)S(1)}, u32[]{:S(2)}, u32[]{:S(2)}) collective-permute-start(f32[512,256]{1,0:T(8,128)S(1)} %get-tuple-element.37), channel_id=1, source_target_pairs={{0,2},{1,3},{2,0},{3,1},{4,6},{5,7},{6,4},{7,5},{8,10},{9,11},{10,... | collective-permute-start | bytes 1572872 | tf_op jit(solution)/shard_map/ppermute | solution.py:209
  51.5 34.5 %all-to-all-start.2 = ((f32[8,6,16,256]{3,2,1,0:T(8,128)}), f32[8,6,16,256]{3,2,1,0:T(8,128)S(1)}, u32[]{:S(2)}, u32[]{:S(2)}) async-start(f32[8,6,16,256]{3,2,1,0:T(8,128)} %broadcast_in_dim.8), calls=%async_computation.2 | async-start | bytes 1572864 | tf_op jit(solution)/shard_map/all_to_all | solution.py:193
  58.4 19.4 %collective-permute-start = (f32[512,256]{1,0:T(8,128)}, f32[512,256]{1,0:T(8,128)S(1)}, u32[]{:S(2)}, u32[]{:S(2)}) collective-permute-start(f32[512,256]{1,0:T(8,128)} %get-tuple-element.32), channel_id=1, source_target_pairs={{0,1},{1,2},{2,3},{3,0},{4,5},{5,6},{6,7},{7,4},{8,9},{9,10},{10,1... | collective-permute-start | bytes 1572872 | tf_op jit(solution)/shard_map/ppermute | solution.py:209
  58.9 22.2 %collective-permute-start.1 = (f32[512,256]{1,0:T(8,128)}, f32[512,256]{1,0:T(8,128)S(1)}, u32[]{:S(2)}, u32[]{:S(2)}) collective-permute-start(f32[512,256]{1,0:T(8,128)} %get-tuple-element.33), channel_id=1, source_target_pairs={{0,3},{1,0},{2,1},{3,2},{4,7},{5,4},{6,5},{7,6},{8,11},{9,8},{10,9... | collective-permute-start | bytes 1572872 | tf_op jit(solution)/shard_map/ppermute | solution.py:209
  60.4 20.7 %collective-permute-start.2 = (f32[512,256]{1,0:T(8,128)}, f32[512,256]{1,0:T(8,128)S(1)}, u32[]{:S(2)}, u32[]{:S(2)}) collective-permute-start(f32[512,256]{1,0:T(8,128)} %get-tuple-element.34), channel_id=1, source_target_pairs={{0,2},{1,3},{2,0},{3,1},{4,6},{5,7},{6,4},{7,5},{8,10},{9,11},{10,... | collective-permute-start | bytes 1572872 | tf_op jit(solution)/shard_map/ppermute | solution.py:209
  61.1 20.9 %collective-permute-start.10 = (f32[8,16,768]{2,1,0:T(8,128)}, f32[8,16,768]{2,1,0:T(8,128)}, u32[]{:S(2)}, u32[]{:S(2)}) collective-permute-start(f32[8,16,768]{2,1,0:T(8,128)} %copy-done.4), channel_id=1, source_target_pairs={{0,128},{4,132},{8,136},{12,140},{16,144},{20,148},{24,152},{28,15... | collective-permute-start | bytes 1179656 | tf_op jit(solution)/shard_map/ppermute | solution.py:205
  62.8 19.2 %collective-permute-start.11 = (f32[8,16,768]{2,1,0:T(8,128)}, f32[8,16,768]{2,1,0:T(8,128)S(1)}, u32[]{:S(2)}, u32[]{:S(2)}) collective-permute-start(f32[8,16,768]{2,1,0:T(8,128)} %copy-done.4), channel_id=1, source_target_pairs={{0,64},{4,68},{8,72},{12,76},{16,80},{20,84},{24,88},{28,92},{32,9... | collective-permute-start | bytes 1179656 | tf_op jit(solution)/shard_map/ppermute | solution.py:205
  77.8 8.1 %collective-permute-start.9 = (f32[8,16,768]{2,1,0:T(8,128)}, f32[8,16,768]{2,1,0:T(8,128)}, u32[]{:S(2)}, u32[]{:S(2)}) collective-permute-start(f32[8,16,768]{2,1,0:T(8,128)} %copy-done.4), channel_id=1, source_target_pairs={{0,192},{4,196},{8,200},{12,204},{16,208},{20,212},{24,216},{28,22... | collective-permute-start | bytes 1179656 | tf_op jit(solution)/shard_map/ppermute | solution.py:205
  85.9 4.9 %collective-permute-start.12 = (f32[8,6,16,256]{3,2,1,0:T(8,128)S(1)}, f32[8,6,16,256]{3,2,1,0:T(8,128)}, u32[]{:S(2)}, u32[]{:S(2)}) collective-permute-start(f32[8,6,16,256]{3,2,1,0:T(8,128)S(1)} %all-to-all-done.2.low_own), channel_id=1, source_target_pairs={{0,4},{4,0},{8,12},{12,8},{16,20},{20,16},{24,28},{28,24},{32,36},... | collective-permute-start | bytes 2359304 | tf_op jit(solution)/shard_map/ppermute | solution.py:199
  85.9 2.8 %collective-permute-start.13 = (f32[8,16,768]{2,1,0:T(8,128)}, f32[8,16,768]{2,1,0:T(8,128)}, u32[]{:S(2)}, u32[]{:S(2)}) collective-permute-start(f32[8,16,768]{2,1,0:T(8,128)} %copy-done.4), channel_id=1, source_target_pairs={{0,4},{4,0},{8,12},{12,8},{16,20},{20,16},{24,28},{28,24},{32,36},... | collective-permute-start | bytes 1179656 | tf_op jit(solution)/shard_map/ppermute | solution.py:199
  86.4 3.2 %collective-permute-start.14 = (f32[8,16,768]{2,1,0:T(8,128)}, f32[8,16,768]{2,1,0:T(8,128)}, u32[]{:S(2)}, u32[]{:S(2)}) collective-permute-start(f32[8,16,768]{2,1,0:T(8,128)} %collective-permute-done.9.refs_1_), channel_id=1, source_target_pairs={{0,4},{4,0},{8,12},{12,8},{16,20},{20,16},{24,28},{28,24},{32,36},... | collective-permute-start | bytes 1179656 | tf_op jit(solution)/shard_map/ppermute | solution.py:199
  86.4 3.8 %collective-permute-start.15 = (f32[8,16,768]{2,1,0:T(8,128)}, f32[8,16,768]{2,1,0:T(8,128)}, u32[]{:S(2)}, u32[]{:S(2)}) collective-permute-start(f32[8,16,768]{2,1,0:T(8,128)} %collective-permute-done.10.refs_2_), channel_id=1, source_target_pairs={{0,4},{4,0},{8,12},{12,8},{16,20},{20,16},{24,28},{28,24},{32,36},... | collective-permute-start | bytes 1179656 | tf_op jit(solution)/shard_map/ppermute | solution.py:199
  86.9 3.9 %collective-permute-start.16 = (f32[8,16,768]{2,1,0:T(8,128)}, f32[8,16,768]{2,1,0:T(8,128)}, u32[]{:S(2)}, u32[]{:S(2)}) collective-permute-start(f32[8,16,768]{2,1,0:T(8,128)} %copy-done.11), channel_id=1, source_target_pairs={{0,4},{4,0},{8,12},{12,8},{16,20},{20,16},{24,28},{28,24},{32,36},... | collective-permute-start | bytes 1179656 | tf_op jit(solution)/shard_map/ppermute | solution.py:199
  87.0 16.4 %copy-start = (f32[4096,256]{1,0:T(8,128)S(1)}, f32[4096,256]{1,0:T(8,128)}, u32[]{:S(2)}) copy-start(f32[4096,256]{1,0:T(8,128)} %own.3) | copy-start | bytes 12582916
  103.4 10.8 %copy-start.10 = (f32[1024,512]{1,0:T(8,128)}, f32[1024,512]{1,0:T(8,128)S(1)}, u32[]{:S(2)}) copy-start(f32[1024,512]{1,0:T(8,128)S(1)} %get-tuple-element.45) | copy-start | bytes 6291460
  103.4 7.9 %copy-start.3 = (f32[512,256]{1,0:T(8,128)S(1)}, f32[512,256]{1,0:T(8,128)}, u32[]{:S(2)}) copy-start(f32[512,256]{1,0:T(8,128)} %copy-done.2) | copy-start | bytes 1572868
  106.3 8.0 %copy-start.6 = (f32[512,128]{1,0:T(8,128)}, f32[512,128]{1,0:T(8,128)S(1)}, u32[]{:S(2)}) copy-start(f32[512,128]{1,0:T(8,128)S(1)} %get-tuple-element.58.own) | copy-start | bytes 786436
  106.3 15.8 %collective-permute-start.20 = (f32[512,128]{1,0:T(8,128)S(1)}, f32[512,128]{1,0:T(8,128)S(1)}, u32[]{:S(2)}, u32[]{:S(2)}) collective-permute-start(f32[512,128]{1,0:T(8,128)S(1)} %get-tuple-element.59), channel_id=1, source_target_pairs={{0,1},{1,2},{2,3},{3,0},{4,5},{5,6},{6,7},{7,4},{8,9},{9,10},{10,1... | collective-permute-start | bytes 786440 | tf_op jit(solution)/shard_map/ppermute | solution.py:209
  109.8 16.3 %collective-permute-start.21 = (f32[512,128]{1,0:T(8,128)}, f32[512,128]{1,0:T(8,128)}, u32[]{:S(2)}, u32[]{:S(2)}) collective-permute-start(f32[512,128]{1,0:T(8,128)} %get-tuple-element.60), channel_id=1, source_target_pairs={{0,3},{1,0},{2,1},{3,2},{4,7},{5,4},{6,5},{7,6},{8,11},{9,8},{10,9... | collective-permute-start | bytes 786440 | tf_op jit(solution)/shard_map/ppermute | solution.py:209
  109.8 16.3 %copy-start.1 = (f32[4096,128]{1,0:T(8,128)S(1)}, f32[4096,128]{1,0:T(8,128)}, u32[]{:S(2)}) copy-start(f32[4096,128]{1,0:T(8,128)} %rhs.3) | copy-start | bytes 6291460
  109.8 16.3 %collective-permute-start.22 = (f32[512,128]{1,0:T(8,128)}, f32[512,128]{1,0:T(8,128)}, u32[]{:S(2)}, u32[]{:S(2)}) collective-permute-start(f32[512,128]{1,0:T(8,128)} %get-tuple-element.61), channel_id=1, source_target_pairs={{0,2},{1,3},{2,0},{3,1},{4,6},{5,7},{6,4},{7,5},{8,10},{9,11},{10,... | collective-permute-start | bytes 786440 | tf_op jit(solution)/shard_map/ppermute | solution.py:209
  115.0 17.7 %collective-permute-start.17 = (f32[512,128]{1,0:T(8,128)}, f32[512,128]{1,0:T(8,128)S(1)}, u32[]{:S(2)}, u32[]{:S(2)}) collective-permute-start(f32[512,128]{1,0:T(8,128)} %get-tuple-element.52), channel_id=1, source_target_pairs={{0,1},{1,2},{2,3},{3,0},{4,5},{5,6},{6,7},{7,4},{8,9},{9,10},{10,1... | collective-permute-start | bytes 786440 | tf_op jit(solution)/shard_map/ppermute | solution.py:209
  116.7 19.4 %collective-permute-start.18 = (f32[512,128]{1,0:T(8,128)}, f32[512,128]{1,0:T(8,128)S(1)}, u32[]{:S(2)}, u32[]{:S(2)}) collective-permute-start(f32[512,128]{1,0:T(8,128)} %get-tuple-element.53), channel_id=1, source_target_pairs={{0,3},{1,0},{2,1},{3,2},{4,7},{5,4},{6,5},{7,6},{8,11},{9,8},{10,9... | collective-permute-start | bytes 786440 | tf_op jit(solution)/shard_map/ppermute | solution.py:209
  122.1 14.1 %collective-permute-start.19 = (f32[512,128]{1,0:T(8,128)}, f32[512,128]{1,0:T(8,128)S(1)}, u32[]{:S(2)}, u32[]{:S(2)}) collective-permute-start(f32[512,128]{1,0:T(8,128)} %get-tuple-element.54), channel_id=1, source_target_pairs={{0,2},{1,3},{2,0},{3,1},{4,6},{5,7},{6,4},{7,5},{8,10},{9,11},{10,... | collective-permute-start | bytes 786440 | tf_op jit(solution)/shard_map/ppermute | solution.py:209
  127.1 9.0 %copy-start.9 = (f32[512,128]{1,0:T(8,128)S(1)}, f32[512,128]{1,0:T(8,128)}, u32[]{:S(2)}) copy-start(f32[512,128]{1,0:T(8,128)} %copy-done.8) | copy-start | bytes 786436
  (7 other events, 6.3 us)
